TPU v7x, 32 devices: a whole 2x2x4 slice. The times are simulated.
32 devices in a mesh: grp: 2 (over x), dom: 16 (over z, y, core).
Axes of the slice: x: 2, y: 2, z: 4, core: 2. Of those that a mesh axis runs over, the one named last changes fastest.
Arguments:
- node_latent: bfloat16 [16384, 128], P(('grp', 'dom')), parts along dimension 0, may hold values from -6 to 6
- edge_latent: bfloat16 [98304, 128], P(('grp', 'dom')), parts along dimension 0, may hold values from -6 to 6
- coarse_edge_latent: bfloat16 [49152, 128], P(('grp', 'dom')), parts along dimension 0, may hold values from -6 to 6
- edge_sender: int32 [98304], P(('grp', 'dom')), parts along dimension 0, may hold values from 0 to 671, as said below
- edge_receiver: int32 [98304], P(('grp', 'dom')), parts along dimension 0, may hold values from -1 to 511, as said below
- halo_list: int32 [5120], P(('grp', 'dom')), parts along dimension 0, may hold values from 0 to 511, as said below
- parent: int32 [16384], P(('grp', 'dom')), parts along dimension 0, may hold values from 0 to 511, as said below
- coarse_sender: int32 [49152], P(('grp', 'dom')), parts along dimension 0, may hold values from 0 to 1535, as said below
- coarse_receiver: int32 [49152], P(('grp', 'dom')), parts along dimension 0, may hold values from 0 to 511
- first_edge_in: bfloat16 [384, 128], replicated, may hold values from -0.3125 to 0.3125
- first_edge_out: bfloat16 [128, 128], replicated, may hold values from -0.5 to 0.5
- first_node_in: bfloat16 [256, 128], replicated, may hold values from -0.375 to 0.375
- first_node_out: bfloat16 [128, 128], replicated, may hold values from -0.5 to 0.5
- coarse_edge_in: bfloat16 [384, 128], replicated, may hold values from -0.3125 to 0.3125
- coarse_edge_out: bfloat16 [128, 128], replicated, may hold values from -0.5 to 0.5
- coarse_node_in: bfloat16 [256, 128], replicated, may hold values from -0.375 to 0.375
- coarse_node_out: bfloat16 [128, 128], replicated, may hold values from -0.5 to 0.5
- second_edge_in: bfloat16 [384, 128], replicated, may hold values from -0.3125 to 0.3125
- second_edge_out: bfloat16 [128, 128], replicated, may hold values from -0.5 to 0.5
- second_node_in: bfloat16 [256, 128], replicated, may hold values from -0.375 to 0.375
- second_node_out: bfloat16 [128, 128], replicated, may hold values from -0.5 to 0.5
Outputs:
- updated_nodes: bfloat16 [16384, 128], P(('grp', 'dom')), parts along dimension 0
There are 2 independent parts, one for each index of `grp`. A program takes and returns all parts, laid end to end along the dimension named above; an argument that names none is the same for every part. Nothing has to cross between parts.
Inputs may be any that keep to these rules, and one draw needn't show every extreme that they name: `edge_receiver`: each partition's 3072 rows hold its live edges first and -1 in every later row; every partition has at least half its rows live, and some partition has no -1. `edge_sender`: indexes the partition's halo table of 672 rows. `halo_list`: Partition-local node numbers. Every coarse node of a block is the parent of at least one fine node of the block's four partitions. `coarse_sender`: indexes the block's coarse table of 1536 rows.
All inputs are finite; a program needn't handle non-finite values.
Results may differ from a plain program's by a relative error of at most 0.012.
Values may be sent and summed in bfloat16 or wider, within the bound.
A program may use at most 64 MiB of HBM per device.

v0:
```python
import jax
import jax.numpy as jnp
from jax import lax
from jax.sharding import PartitionSpec as P


def shifted_2(value, axis, steps):
    count = lax.axis_size(axis)
    pairs = [(source, (source + steps) % count) for source in range(count)]
    return lax.ppermute(value, axis, pairs)


def swapped(block, axis, bit):
    count = lax.axis_size(axis)
    route = []
    for low in range(count):
        high = low | 1 << bit
        if high != low and high < count:
            route += [(low, high), (high, low)]
    return lax.ppermute(block, axis, route)


def layer_norm(values):
    centre = jnp.mean(values, axis=-1, keepdims=True)
    shifted = values - centre
    spread = jnp.mean(shifted * shifted, axis=-1, keepdims=True)
    return shifted * lax.rsqrt(spread + 1e-05)


def edge_pass(node_rows, table, edge_rows, senders, receivers, weight_in, weight_out):
    node_count, row_width = node_rows.shape
    target = jnp.where(receivers < 0, node_count, receivers)
    padded = jnp.concatenate([node_rows, jnp.zeros((1, row_width), node_rows.dtype)], axis=0)
    sender_rows = jnp.take(table, senders, axis=0)
    receiver_rows = jnp.take(padded, target, axis=0)
    linear = jnp.dot(edge_rows, weight_in[:row_width], preferred_element_type=jnp.float32)
    linear = linear + jnp.dot(
        sender_rows, weight_in[row_width : 2 * row_width], preferred_element_type=jnp.float32
    )
    linear = linear + jnp.dot(
        receiver_rows, weight_in[2 * row_width :], preferred_element_type=jnp.float32
    )
    hidden = jax.nn.silu(linear).astype(jnp.bfloat16)
    normed = layer_norm(jnp.dot(hidden, weight_out, preferred_element_type=jnp.float32))
    new_edges = (edge_rows.astype(jnp.float32) + normed).astype(jnp.bfloat16)
    summed = jax.ops.segment_sum(
        new_edges.astype(jnp.float32), target, num_segments=node_count + 1
    )[:node_count]
    return (new_edges, summed)


def node_pass(node_rows, summed, weight_in, weight_out):
    row_width = node_rows.shape[1]
    linear = jnp.dot(node_rows, weight_in[:row_width], preferred_element_type=jnp.float32)
    linear = linear + jnp.dot(
        summed.astype(jnp.bfloat16), weight_in[row_width:], preferred_element_type=jnp.float32
    )
    hidden = jax.nn.silu(linear).astype(jnp.bfloat16)
    normed = layer_norm(jnp.dot(hidden, weight_out, preferred_element_type=jnp.float32))
    return (node_rows.astype(jnp.float32) + normed).astype(jnp.bfloat16)


def halo_table(node_rows, halo_list):
    slot_rows = halo_list.shape[0] // 5
    device_count = lax.axis_size("dom")
    offsets = (1, -1, 2, -2, device_count // 2)
    outgoing = [
        jnp.take(node_rows, halo_list[number * slot_rows : (number + 1) * slot_rows], axis=0)
        for number in range(5)
    ]
    received = [shifted_2(outgoing[number], "dom", offset) for number, offset in enumerate(offsets)]
    return jnp.concatenate([node_rows] + received, axis=0)


def pool_nodes(node_rows, parent):
    node_count = node_rows.shape[0]
    pooled_sum = jax.ops.segment_sum(node_rows.astype(jnp.float32), parent, num_segments=node_count)
    child_count = jax.ops.segment_sum(
        jnp.ones(parent.shape, jnp.float32), parent, num_segments=node_count
    )
    for bit_number in (0, 1):
        partner = (
            swapped(pooled_sum.astype(jnp.bfloat16), "dom", bit_number).astype(pooled_sum.dtype),
            swapped(child_count.astype(jnp.bfloat16), "dom", bit_number).astype(child_count.dtype),
        )
        pooled_sum = pooled_sum + partner[0]
        child_count = child_count + partner[1]
    return (pooled_sum / child_count[:, None]).astype(jnp.bfloat16)


def coarse_finish(coarse_rows, coarse_summed, weight_in, weight_out):
    for bit_number in (0, 1):
        coarse_summed = coarse_summed + swapped(
            coarse_summed.astype(jnp.bfloat16), "dom", bit_number
        ).astype(coarse_summed.dtype)
    return node_pass(coarse_rows, coarse_summed, weight_in, weight_out)


def on_device(
    node_latent,
    edge_latent,
    coarse_edge_latent,
    edge_sender,
    edge_receiver,
    halo_list,
    parent,
    coarse_sender,
    coarse_receiver,
    first_edge_in,
    first_edge_out,
    first_node_in,
    first_node_out,
    coarse_edge_in,
    coarse_edge_out,
    coarse_node_in,
    coarse_node_out,
    second_edge_in,
    second_edge_out,
    second_node_in,
    second_node_out,
):
    table = halo_table(node_latent, halo_list)
    first_edges, summed = edge_pass(
        node_latent, table, edge_latent, edge_sender, edge_receiver, first_edge_in, first_edge_out
    )
    first_nodes = node_pass(node_latent, summed, first_node_in, first_node_out)
    coarse_rows = pool_nodes(first_nodes, parent)
    coarse_table = jnp.concatenate(
        [coarse_rows] + [shifted_2(coarse_rows, "dom", offset) for offset in (4, -4)], axis=0
    )
    coarse_edges_new, coarse_summed = edge_pass(
        coarse_rows,
        coarse_table,
        coarse_edge_latent,
        coarse_sender,
        coarse_receiver,
        coarse_edge_in,
        coarse_edge_out,
    )
    coarse_new = coarse_finish(coarse_rows, coarse_summed, coarse_node_in, coarse_node_out)
    lifted = jnp.take(coarse_new, parent, axis=0)
    middle_nodes = (first_nodes.astype(jnp.float32) + lifted.astype(jnp.float32)).astype(
        jnp.bfloat16
    )
    table = halo_table(middle_nodes, halo_list)
    second_edges, summed = edge_pass(
        middle_nodes,
        table,
        first_edges,
        edge_sender,
        edge_receiver,
        second_edge_in,
        second_edge_out,
    )
    return node_pass(middle_nodes, summed, second_node_in, second_node_out)


def solution(mesh):
    placed = (
        P(("grp", "dom"), None),
        P(("grp", "dom"), None),
        P(("grp", "dom"), None),
        P(("grp", "dom")),
        P(("grp", "dom")),
        P(("grp", "dom")),
        P(("grp", "dom")),
        P(("grp", "dom")),
        P(("grp", "dom")),
        P(),
        P(),
        P(),
        P(),
        P(),
        P(),
        P(),
        P(),
        P(),
        P(),
        P(),
        P(),
    )
    return jax.shard_map(
        on_device, mesh=mesh, in_specs=placed, out_specs=P(("grp", "dom"), None), check_vma=False
    )
```

profile of v0, /device:TPU:0, one launch (start us, length us, event | category | flops | bytes accessed | tf_op | source)
XLA Modules:
  0.0 196.5 jit_solution(8556672971913482362)
XLA Ops:
  0.0 0.9 compare_and_fusion.4
  1.0 1.5 gather_fusion.3
  3.0 1.5 gather_fusion.4
  4.6 5.0 %collective-permute-start.1 = (bf16[32,128]{1,0:T(8,128)(2,1)S(1)}, bf16[32,128]{1,0:T(8,128)(2,1)S(1)}, u32[]{:S(2)}, u32[]{:S(2)}) collective-permute-start(bf16[32,128]{1,0:T(8,128)(2,1)S(1)} %broadcast_select_fusion.7), channel_id=1, source_target_pairs={{0,15},{1,0},{2,1},{3,2},{4,3},{5,4},{6,5},{7,6},{8,7},{9,8},{10,9... | collective-permute-start | bytes 24584 | tf_op jit(solution)/shard_map/ppermute | solution.py:10
  9.6 1.5 gather_fusion.5
  11.2 1.5 gather_fusion.6
  12.8 4.7 %collective-permute-start.3 = (bf16[32,128]{1,0:T(8,128)(2,1)S(1)}, bf16[32,128]{1,0:T(8,128)(2,1)S(1)}, u32[]{:S(2)}, u32[]{:S(2)}) collective-permute-start(bf16[32,128]{1,0:T(8,128)(2,1)S(1)} %broadcast_select_fusion.3), channel_id=1, source_target_pairs={{0,14},{1,15},{2,0},{3,1},{4,2},{5,3},{6,4},{7,5},{8,6},{9,7},{10,... | collective-permute-start | bytes 24584 | tf_op jit(solution)/shard_map/ppermute | solution.py:10
  17.5 1.5 gather_fusion.7
  19.1 0.7 fusion.80
  19.8 0.7 compare_and_fusion.1
  20.5 0.7 fusion.81
  21.3 1.3 compare_and_fusion
  22.6 0.7 compare_select_fusion.4
  23.3 0.7 compare_and_fusion.3
  24.0 0.7 compare_select_fusion.3
  24.7 1.3 compare_and_fusion.2
  25.9 1.8 fusion.78
  27.7 0.7 compare_select_fusion.6
  28.4 1.1 fusion.76
  29.5 1.2 fusion.67
  30.8 2.3 %copy.28 = bf16[3072,128]{0,1:T(8,128)(2,1)} copy(bf16[3072,128]{1,0:T(8,128)(2,1)} %param.28) | data formatting | bytes 1572864 | tf_op args[1]
  33.2 4.1 %scatter_custom_fusion.2 = f32[512]{0:T(512)S(1)} fusion(s32[512]{0:T(512)S(1)} %copy-done.14, f32[512]{0:T(512)S(1)} %broadcast.165, f32[]{:T(128)} %constant.81.clone.1), kind=kCustom, calls=%fused_computation.189 | custom fusion | flops 512 | bytes 2052 | tf_op jit(solution)/shard_map/scatter-add | solution.py:78
  37.8 11.5 %gather_fusion.9 = bf16[3072,128]{1,0:T(8,128)(2,1)} fusion(bf16[513,128]{1,0:T(8,128)(2,1)S(1)} %concatenate.19, s32[3072]{0:T(1024)S(1)} %get-tuple-element.20), kind=kCustom, calls=%fused_computation.2.clone | custom fusion | bytes 1585152 | tf_op jit(solution)/shard_map/jit(_take)/gather | solution.py:35
  49.4 11.5 %gather_fusion.8 = bf16[3072,128]{1,0:T(8,128)(2,1)} fusion(bf16[672,128]{1,0:T(8,128)(2,1)S(1)} %constant_dynamic-update-slice_fusion, s32[3072]{0:T(1024)S(1)} %fusion.80), kind=kCustom, calls=%fused_computation.1.clone | custom fusion | bytes 1585152 | tf_op jit(solution)/shard_map/jit(_take)/gather | solution.py:34
  60.9 3.0 %convolution_add_fusion.3 = f32[3072,128]{1,0:T(8,128)} fusion(f32[3072,128]{1,0:T(8,128)S(1)} %fusion.76, bf16[3072,128]{1,0:T(8,128)(2,1)} %gather_fusion.8, pred[3072]{0:T(1024)(128)(4,1)S(1)} %compare_and_fusion.1, bf16[384,128]{1,0:T(8,128)(2,1)S(1)} %copy-done.8), kind=kOutput, calls=%fused_computation.25 | convolution fusion | flops 101449728 | bytes 3968000 | tf_op jit(solution)/shard_map/dot_general | solution.py:37
  63.9 2.3 %fusion.101 = (f32[3072]{0:T(1024)S(1)}, f32[3072,128]{0,1:T(8,128)S(1)}) fusion(bf16[128,128]{1,0:T(8,128)(2,1)S(1)} %copy-done, f32[3072,128]{1,0:T(8,128)} %convolution_add_fusion.3, bf16[3072,128]{1,0:T(8,128)(2,1)S(1)} %copy-done.5, pred[3072]{0:T(1024)(128)(4,1)S(1)} %copy-done.21, bf16[384,128]{1,0:T(8,128)(2,1)S(1)} %copy-done.8), kind=kOutput, calls=%fused_computation.206 | convolution fusion | flops 204469248 | bytes 4013056 | tf_op jit(solution)/shard_map/dot_general | solution.py:44
  66.4 0.9 copy-done.3
  67.9 17.6 %scatter_custom_fusion = f32[513,128]{1,0:T(8,128)} fusion(s32[3072]{0:T(1024)S(1)} %get-tuple-element.21, f32[3072,128]{1,0:T(8,128)S(1)} %copy.29, f32[]{:T(128)} %constant.81.clone.1), kind=kCustom, calls=%fused_computation.96 | custom fusion | flops 393216 | bytes 262660 | tf_op jit(solution)/shard_map/scatter-add | solution.py:46
  85.5 1.5 fusion.106
  87.4 2.3 %scatter_custom_fusion.1 = f32[512,128]{1,0:T(8,128)S(1)} fusion(s32[512]{0:T(512)S(1)} %copy-done.14, bf16[512,128]{1,0:T(8,128)(2,1)S(1)} %add_convert_fusion.6, f32[]{:T(128)} %constant.81.clone.1), kind=kCustom, calls=%fused_computation.66 | custom fusion | flops 131072 | bytes 393220 | tf_op jit(solution)/shard_map/scatter-add | solution.py:77
  89.9 3.0 %collective-permute-start.5 = (bf16[512,128]{0,1:T(8,128)(2,1)S(1)}, bf16[512,128]{0,1:T(8,128)(2,1)S(1)}, u32[]{:S(2)}, u32[]{:S(2)}) collective-permute-start(bf16[512,128]{0,1:T(8,128)(2,1)S(1)} %convert_element_type.123), channel_id=1, source_target_pairs={{0,1},{1,0},{2,3},{3,2},{4,5},{5,4},{6,7},{7,6},{8,9},{9,8},{10,11... | collective-permute-start | bytes 393224 | tf_op jit(solution)/shard_map/ppermute | solution.py:20
  92.9 0.6 fusion.82
  93.9 1.8 collective-permute-start.6
  95.7 1.4 collective-permute-done.8
  97.1 0.6 convert_add_fusion.3
  97.8 2.0 %collective-permute-done.6 = bf16[512,128]{0,1:T(8,128)(2,1)S(1)} collective-permute-done((bf16[512,128]{0,1:T(8,128)(2,1)S(1)}, bf16[512,128]{0,1:T(8,128)(2,1)S(1)}, u32[]{:S(2)}, u32[]{:S(2)}) %collective-permute-start.6) | collective-permute-done | bytes 131104 | tf_op jit(solution)/shard_map/ppermute | solution.py:20
  99.8 0.8 collective-permute-start.10
  100.6 1.3 collective-permute-start.9
  102.3 4.1 %gather_fusion.1 = bf16[1536,128]{1,0:T(8,128)(2,1)} fusion(bf16[513,128]{1,0:T(8,128)(2,1)S(1)} %concatenate.21.clone, s32[2048]{0:T(1024)S(1)} %pad_clamp_fusion), kind=kCustom, calls=%fused_computation.15 | custom fusion | bytes 792576 | tf_op jit(solution)/shard_map/jit(_take)/gather | solution.py:35
  106.3 2.3 %collective-permute-done.9 = bf16[512,128]{0,1:T(8,128)(2,1)S(1)} collective-permute-done((bf16[512,128]{0,1:T(8,128)(2,1)S(1)}, bf16[512,128]{0,1:T(8,128)(2,1)S(1)}, u32[]{:S(2)}, u32[]{:S(2)}) %collective-permute-start.9) | collective-permute-done | bytes 131104 | tf_op jit(solution)/shard_map/ppermute | solution.py:10
  108.9 3.2 %gather_fusion = bf16[1536,128]{1,0:T(8,128)(2,1)S(1)} fusion(bf16[1536,128]{1,0:T(8,128)(2,1)S(1)} %copy.33, s32[2048]{0:T(1024)S(1)} %pad_clamp_fusion.1), kind=kCustom, calls=%fused_computation.14 | custom fusion | bytes 792576 | tf_op jit(solution)/shard_map/jit(_take)/gather | solution.py:34
  112.1 1.3 convolution_add_fusion.5
  113.4 1.7 fusion.109
  115.7 8.8 %scatter_custom_fusion.3 = f32[513,128]{1,0:T(8,128)S(1)} fusion(s32[1536]{0:T(1024)S(1)} %get-tuple-element.23, f32[1536,128]{1,0:T(8,128)S(1)} %copy.35, f32[]{:T(128)} %constant.81.clone.1), kind=kCustom, calls=%fused_computation.94 | custom fusion | flops 196608 | bytes 262660 | tf_op jit(solution)/shard_map/scatter-add | solution.py:46
  124.6 1.3 collective-permute-done.11
  126.0 1.3 collective-permute-start.12
  127.2 1.2 fusion.59
  128.4 3.2 %collective-permute-done.12 = bf16[512,128]{1,0:T(8,128)(2,1)S(1)} collective-permute-done((bf16[512,128]{1,0:T(8,128)(2,1)S(1)}, bf16[512,128]{1,0:T(8,128)(2,1)S(1)}, u32[]{:S(2)}, u32[]{:S(2)}) %collective-permute-start.12) | collective-permute-done | bytes 131104 | tf_op jit(solution)/shard_map/ppermute | solution.py:20
  132.5 1.3 gather_fusion.2
  134.0 0.6 gather_fusion.10
  134.6 0.6 gather_fusion.11
  135.8 0.6 gather_fusion.13
  136.4 0.6 gather_fusion.14
  137.2 4.4 %collective-permute-start.14 = (bf16[32,128]{1,0:T(8,128)(2,1)S(1)}, bf16[32,128]{1,0:T(8,128)(2,1)S(1)}, u32[]{:S(2)}, u32[]{:S(2)}) collective-permute-start(bf16[32,128]{1,0:T(8,128)(2,1)S(1)} %broadcast_select_fusion.6), channel_id=1, source_target_pairs={{0,15},{1,0},{2,1},{3,2},{4,3},{5,4},{6,5},{7,6},{8,7},{9,8},{10,9... | collective-permute-start | bytes 24584 | tf_op jit(solution)/shard_map/ppermute | solution.py:10
  141.7 4.7 %collective-permute-start.16 = (bf16[32,128]{1,0:T(8,128)(2,1)S(1)}, bf16[32,128]{1,0:T(8,128)(2,1)S(1)}, u32[]{:S(2)}, u32[]{:S(2)}) collective-permute-start(bf16[32,128]{1,0:T(8,128)(2,1)S(1)} %broadcast_select_fusion.2), channel_id=1, source_target_pairs={{0,14},{1,15},{2,0},{3,1},{4,2},{5,3},{6,4},{7,5},{8,6},{9,7},{10,... | collective-permute-start | bytes 24584 | tf_op jit(solution)/shard_map/ppermute | solution.py:10
  146.5 0.9 fusion.61
  147.4 11.5 %gather_fusion.16 = bf16[3072,128]{1,0:T(8,128)(2,1)} fusion(bf16[513,128]{1,0:T(8,128)(2,1)S(1)} %concatenate.23, s32[3072]{0:T(1024)S(1)} %get-tuple-element.20), kind=kCustom, calls=%fused_computation.13.clone | custom fusion | bytes 1585152 | tf_op jit(solution)/shard_map/jit(_take)/gather | solution.py:35
  159.1 9.2 %gather_fusion.15 = bf16[3072,128]{1,0:T(8,128)(2,1)S(1)} fusion(bf16[672,128]{1,0:T(8,128)(2,1)S(1)} %constant_dynamic-update-slice_fusion.6, s32[3072]{0:T(1024)S(1)} %fusion.80), kind=kCustom, calls=%fused_computation.12.clone | custom fusion | bytes 1585152 | tf_op jit(solution)/shard_map/jit(_take)/gather | solution.py:34
  168.3 3.5 %convolution_add_fusion.1 = f32[3072,128]{1,0:T(8,128)} fusion(f32[3072,128]{1,0:T(8,128)S(1)} %fusion.59, bf16[3072,128]{1,0:T(8,128)(2,1)S(1)} %gather_fusion.15, pred[3072]{0:T(1024)(128)(4,1)S(1)} %compare_and_fusion.1, bf16[384,128]{1,0:T(8,128)(2,1)} %param.44), kind=kOutput, calls=%fused_computation.23 | convolution fusion | flops 101449728 | bytes 3968000 | tf_op jit(solution)/shard_map/dot_general | solution.py:37
  171.7 2.5 %fusion.117 = (f32[3072]{0:T(1024)S(1)}, f32[3072,128]{0,1:T(8,128)S(1)}) fusion(bf16[128,128]{1,0:T(8,128)(2,1)S(1)} %copy-done.27, f32[3072,128]{1,0:T(8,128)} %convolution_add_fusion.1, bf16[3072,128]{1,0:T(8,128)(2,1)} %gather_fusion.16, pred[3072]{0:T(1024)(128)(4,1)S(1)} %copy-done.22, bf16[384,128]{1,0:T(8,128)(2,1)} %param.44), kind=kOutput, calls=%fused_computation.210 | convolution fusion | flops 204469248 | bytes 4013056 | tf_op jit(solution)/shard_map/dot_general | solution.py:44
  174.5 1.4 fusion.2
  175.9 1.9 copy.37
  177.8 16.9 %scatter_custom_fusion.4 = f32[513,128]{1,0:T(8,128)S(1)} fusion(s32[3072]{0:T(1024)S(1)} %get-tuple-element.21, f32[3072,128]{1,0:T(8,128)S(1)} %copy.37, f32[]{:T(128)} %constant.81.clone.1), kind=kCustom, calls=%fused_computation.92 | custom fusion | flops 393216 | bytes 262660 | tf_op jit(solution)/shard_map/scatter-add | solution.py:46
  195.6 0.9 add_convert_fusion.3
  (155 shorter events, 7.6 us)
Async XLA Ops:
  0.0 63.9 %copy-start = (bf16[128,128]{1,0:T(8,128)(2,1)S(1)}, bf16[128,128]{1,0:T(8,128)(2,1)}, u32[]{:S(2)}) copy-start(bf16[128,128]{1,0:T(8,128)(2,1)} %param.37) | copy-start | bytes 98308
  0.0 28.4 %copy-start.2 = (bf16[3072,128]{1,0:T(8,128)(2,1)S(1)}, bf16[3072,128]{1,0:T(8,128)(2,1)}, u32[]{:S(2)}) copy-start(bf16[3072,128]{1,0:T(8,128)(2,1)} %param.28) | copy-start | bytes 2359300
  0.9 2.1 %copy-start.19 = (pred[32]{0:T(512)(128)(4,1)}, pred[32]{0:T(512)(128)(4,1)S(1)}, u32[]{:S(2)}) copy-start(pred[32]{0:T(512)(128)(4,1)S(1)} %get-tuple-element.28) | copy-start | bytes 100
  1.0 8.7 %copy-start.17 = (pred[32]{0:T(512)(128)(4,1)}, pred[32]{0:T(512)(128)(4,1)S(1)}, u32[]{:S(2)}) copy-start(pred[32]{0:T(512)(128)(4,1)S(1)} %get-tuple-element.26) | copy-start | bytes 100
  1.0 10.3 %copy-start.15 = (pred[32]{0:T(512)(128)(4,1)}, pred[32]{0:T(512)(128)(4,1)S(1)}, u32[]{:S(2)}) copy-start(pred[32]{0:T(512)(128)(4,1)S(1)} %get-tuple-element.24) | copy-start | bytes 100
  2.6 46.8 %collective-permute-start = (bf16[32,128]{1,0:T(8,128)(2,1)S(1)}, bf16[32,128]{1,0:T(8,128)(2,1)S(1)}, u32[]{:S(2)}, u32[]{:S(2)}) collective-permute-start(bf16[32,128]{1,0:T(8,128)(2,1)S(1)} %broadcast_select_fusion.9), channel_id=1, source_target_pairs={{0,1},{1,2},{2,3},{3,4},{4,5},{5,6},{6,7},{7,8},{8,9},{9,10},{10,1... | collective-permute-start | bytes 24584 | tf_op jit(solution)/shard_map/ppermute | solution.py:10
  4.6 44.7 %collective-permute-start.1 = (bf16[32,128]{1,0:T(8,128)(2,1)S(1)}, bf16[32,128]{1,0:T(8,128)(2,1)S(1)}, u32[]{:S(2)}, u32[]{:S(2)}) collective-permute-start(bf16[32,128]{1,0:T(8,128)(2,1)S(1)} %broadcast_select_fusion.7), channel_id=1, source_target_pairs={{0,15},{1,0},{2,1},{3,2},{4,3},{5,4},{6,5},{7,6},{8,7},{9,8},{10,9... | collective-permute-start | bytes 24584 | tf_op jit(solution)/shard_map/ppermute | solution.py:10
  11.2 38.1 %collective-permute-start.2 = (bf16[32,128]{1,0:T(8,128)(2,1)S(1)}, bf16[32,128]{1,0:T(8,128)(2,1)S(1)}, u32[]{:S(2)}, u32[]{:S(2)}) collective-permute-start(bf16[32,128]{1,0:T(8,128)(2,1)S(1)} %broadcast_select_fusion.5), channel_id=1, source_target_pairs={{0,2},{1,3},{2,4},{3,5},{4,6},{5,7},{6,8},{7,9},{8,10},{9,11},{10,... | collective-permute-start | bytes 24584 | tf_op jit(solution)/shard_map/ppermute | solution.py:10
  12.8 36.6 %collective-permute-start.3 = (bf16[32,128]{1,0:T(8,128)(2,1)S(1)}, bf16[32,128]{1,0:T(8,128)(2,1)S(1)}, u32[]{:S(2)}, u32[]{:S(2)}) collective-permute-start(bf16[32,128]{1,0:T(8,128)(2,1)S(1)} %broadcast_select_fusion.3), channel_id=1, source_target_pairs={{0,14},{1,15},{2,0},{3,1},{4,2},{5,3},{6,4},{7,5},{8,6},{9,7},{10,... | collective-permute-start | bytes 24584 | tf_op jit(solution)/shard_map/ppermute | solution.py:10
  19.1 30.3 %collective-permute-start.4 = (bf16[32,128]{1,0:T(8,128)(2,1)S(1)}, bf16[32,128]{1,0:T(8,128)(2,1)S(1)}, u32[]{:S(2)}, u32[]{:S(2)}) collective-permute-start(bf16[32,128]{1,0:T(8,128)(2,1)S(1)} %broadcast_select_fusion.1), channel_id=1, source_target_pairs={{0,8},{1,9},{2,10},{3,11},{4,12},{5,13},{6,14},{7,15},{8,0},{9,1},... | collective-permute-start | bytes 24584 | tf_op jit(solution)/shard_map/ppermute | solution.py:10
  28.4 2.4 %copy-start.1 = (bf16[512,128]{1,0:T(8,128)(2,1)S(1)}, bf16[512,128]{1,0:T(8,128)(2,1)}, u32[]{:S(2)}) copy-start(bf16[512,128]{1,0:T(8,128)(2,1)} %param.27) | copy-start | bytes 393220
  29.5 3.6 %copy-start.14 = (s32[512]{0:T(512)S(1)}, s32[512]{0:T(512)}, u32[]{:S(2)}) copy-start(s32[512]{0:T(512)} %param.33) | copy-start | bytes 6148
  49.3 43.6 %collective-permute-start.7 = (bf16[512]{0:T(512)(128)(2,1)}, bf16[512]{0:T(512)(128)(2,1)}, u32[]{:S(2)}, u32[]{:S(2)}) collective-permute-start(bf16[512]{0:T(512)(128)(2,1)} %convert_element_type.127), channel_id=1, source_target_pairs={{0,1},{1,0},{2,3},{3,2},{4,5},{5,4},{6,7},{7,6},{8,9},{9,8},{10,11... | collective-permute-start | bytes 3080 | tf_op jit(solution)/shard_map/ppermute | solution.py:20
  49.4 11.5 %copy-start.8 = (bf16[384,128]{1,0:T(8,128)(2,1)S(1)}, bf16[384,128]{1,0:T(8,128)(2,1)}, u32[]{:S(2)}) copy-start(bf16[384,128]{1,0:T(8,128)(2,1)} %param.36) | copy-start | bytes 294916
  60.9 3.0 %copy-start.5 = (bf16[3072,128]{1,0:T(8,128)(2,1)S(1)}, bf16[3072,128]{1,0:T(8,128)(2,1)}, u32[]{:S(2)}) copy-start(bf16[3072,128]{1,0:T(8,128)(2,1)} %gather_fusion.9) | copy-start | bytes 2359300
  60.9 3.0 %copy-start.21 = (pred[3072]{0:T(1024)(128)(4,1)S(1)}, pred[3072]{0:T(1024)(128)(4,1)}, u32[]{:S(2)}) copy-start(pred[3072]{0:T(1024)(128)(4,1)} %compare_and_fusion) | copy-start | bytes 9220
  66.2 1.1 copy-start.3
  67.6 17.9 %copy-start.11 = (bf16[256,128]{1,0:T(8,128)(2,1)S(1)}, bf16[256,128]{1,0:T(8,128)(2,1)}, u32[]{:S(2)}) copy-start(bf16[256,128]{1,0:T(8,128)(2,1)} %param.38) | copy-start | bytes 196612
  67.6 17.9 %copy-start.24 = (bf16[128,128]{1,0:T(8,128)(2,1)S(1)}, bf16[128,128]{1,0:T(8,128)(2,1)}, u32[]{:S(2)}) copy-start(bf16[128,128]{1,0:T(8,128)(2,1)} %param.39) | copy-start | bytes 98308
  87.2 14.7 %copy-start.4 = (bf16[1536,128]{1,0:T(8,128)(2,1)S(1)}, bf16[1536,128]{1,0:T(8,128)(2,1)}, u32[]{:S(2)}) copy-start(bf16[1536,128]{1,0:T(8,128)(2,1)} %param.29) | copy-start | bytes 1179652
  89.9 4.0 %collective-permute-start.5 = (bf16[512,128]{0,1:T(8,128)(2,1)S(1)}, bf16[512,128]{0,1:T(8,128)(2,1)S(1)}, u32[]{:S(2)}, u32[]{:S(2)}) collective-permute-start(bf16[512,128]{0,1:T(8,128)(2,1)S(1)} %convert_element_type.123), channel_id=1, source_target_pairs={{0,1},{1,0},{2,3},{3,2},{4,5},{5,4},{6,7},{7,6},{8,9},{9,8},{10,11... | collective-permute-start | bytes 393224 | tf_op jit(solution)/shard_map/ppermute | solution.py:20
  93.6 3.6 %collective-permute-start.8 = (bf16[512]{0:T(512)(128)(2,1)S(1)}, bf16[512]{0:T(512)(128)(2,1)S(1)}, u32[]{:S(2)}, u32[]{:S(2)}) collective-permute-start(bf16[512]{0:T(512)(128)(2,1)S(1)} %fusion.82), channel_id=1, source_target_pairs={{0,2},{2,0},{1,3},{3,1},{4,6},{6,4},{5,7},{7,5},{8,10},{10,8},{9,1... | collective-permute-start | bytes 3080 | tf_op jit(solution)/shard_map/ppermute | solution.py:20
  93.9 5.8 %collective-permute-start.6 = (bf16[512,128]{0,1:T(8,128)(2,1)S(1)}, bf16[512,128]{0,1:T(8,128)(2,1)S(1)}, u32[]{:S(2)}, u32[]{:S(2)}) collective-permute-start(bf16[512,128]{0,1:T(8,128)(2,1)S(1)} %fusion.41), channel_id=1, source_target_pairs={{0,2},{2,0},{1,3},{3,1},{4,6},{6,4},{5,7},{7,5},{8,10},{10,8},{9,1... | collective-permute-start | bytes 393224 | tf_op jit(solution)/shard_map/ppermute | solution.py:20
  99.8 6.5 %collective-permute-start.10 = (bf16[512,128]{0,1:T(8,128)(2,1)S(1)}, bf16[512,128]{0,1:T(8,128)(2,1)S(1)}, u32[]{:S(2)}, u32[]{:S(2)}) collective-permute-start(bf16[512,128]{0,1:T(8,128)(2,1)S(1)} %divide_convert_fusion), channel_id=1, source_target_pairs={{0,12},{1,13},{2,14},{3,15},{4,0},{5,1},{6,2},{7,3},{8,4},{9,5},{1... | collective-permute-start | bytes 393224 | tf_op jit(solution)/shard_map/ppermute | solution.py:10
  100.6 8.0 %collective-permute-start.9 = (bf16[512,128]{0,1:T(8,128)(2,1)S(1)}, bf16[512,128]{0,1:T(8,128)(2,1)S(1)}, u32[]{:S(2)}, u32[]{:S(2)}) collective-permute-start(bf16[512,128]{0,1:T(8,128)(2,1)S(1)} %divide_convert_fusion), channel_id=1, source_target_pairs={{0,4},{1,5},{2,6},{3,7},{4,8},{5,9},{6,10},{7,11},{8,12},{9,13},{1... | collective-permute-start | bytes 393224 | tf_op jit(solution)/shard_map/ppermute | solution.py:10
  108.9 3.2 %copy-start.9 = (bf16[384,128]{1,0:T(8,128)(2,1)S(1)}, bf16[384,128]{1,0:T(8,128)(2,1)}, u32[]{:S(2)}) copy-start(bf16[384,128]{1,0:T(8,128)(2,1)} %param.40) | copy-start | bytes 294916
  112.1 1.3 copy-start.6
  112.1 1.3 copy-start.23
  112.1 1.3 copy-start.25
  124.5 7.1 %copy-start.10 = (bf16[256,128]{1,0:T(8,128)(2,1)S(1)}, bf16[256,128]{1,0:T(8,128)(2,1)}, u32[]{:S(2)}) copy-start(bf16[256,128]{1,0:T(8,128)(2,1)} %param.42) | copy-start | bytes 196612
  124.5 1.4 collective-permute-start.11
  126.0 5.8 %copy-start.26 = (bf16[128,128]{1,0:T(8,128)(2,1)S(1)}, bf16[128,128]{1,0:T(8,128)(2,1)}, u32[]{:S(2)}) copy-start(bf16[128,128]{1,0:T(8,128)(2,1)} %param.43) | copy-start | bytes 98308
  126.0 5.6 %collective-permute-start.12 = (bf16[512,128]{1,0:T(8,128)(2,1)S(1)}, bf16[512,128]{1,0:T(8,128)(2,1)S(1)}, u32[]{:S(2)}, u32[]{:S(2)}) collective-permute-start(bf16[512,128]{1,0:T(8,128)(2,1)S(1)} %fusion.42), channel_id=1, source_target_pairs={{0,2},{2,0},{1,3},{3,1},{4,6},{6,4},{5,7},{7,5},{8,10},{10,8},{9,1... | collective-permute-start | bytes 393224 | tf_op jit(solution)/shard_map/ppermute | solution.py:20
  132.2 4.8 %copy-start.20 = (pred[32]{0:T(512)(128)(4,1)S(1)}, pred[32]{0:T(512)(128)(4,1)}, u32[]{:S(2)}) copy-start(pred[32]{0:T(512)(128)(4,1)} %copy-done.19) | copy-start | bytes 100
  132.2 4.8 %copy-start.18 = (pred[32]{0:T(512)(128)(4,1)S(1)}, pred[32]{0:T(512)(128)(4,1)}, u32[]{:S(2)}) copy-start(pred[32]{0:T(512)(128)(4,1)} %copy-done.17) | copy-start | bytes 100
  132.3 9.3 %copy-start.16 = (pred[32]{0:T(512)(128)(4,1)S(1)}, pred[32]{0:T(512)(128)(4,1)}, u32[]{:S(2)}) copy-start(pred[32]{0:T(512)(128)(4,1)} %copy-done.15) | copy-start | bytes 100
  132.3 14.3 %copy-start.12 = (bf16[256,128]{1,0:T(8,128)(2,1)S(1)}, bf16[256,128]{1,0:T(8,128)(2,1)}, u32[]{:S(2)}) copy-start(bf16[256,128]{1,0:T(8,128)(2,1)} %param.46) | copy-start | bytes 196612
  137.1 21.9 %collective-permute-start.13 = (bf16[32,128]{1,0:T(8,128)(2,1)S(1)}, bf16[32,128]{1,0:T(8,128)(2,1)S(1)}, u32[]{:S(2)}, u32[]{:S(2)}) collective-permute-start(bf16[32,128]{1,0:T(8,128)(2,1)S(1)} %broadcast_select_fusion.8), channel_id=1, source_target_pairs={{0,1},{1,2},{2,3},{3,4},{4,5},{5,6},{6,7},{7,8},{8,9},{9,10},{10,1... | collective-permute-start | bytes 24584 | tf_op jit(solution)/shard_map/ppermute | solution.py:10
  137.2 21.8 %collective-permute-start.14 = (bf16[32,128]{1,0:T(8,128)(2,1)S(1)}, bf16[32,128]{1,0:T(8,128)(2,1)S(1)}, u32[]{:S(2)}, u32[]{:S(2)}) collective-permute-start(bf16[32,128]{1,0:T(8,128)(2,1)S(1)} %broadcast_select_fusion.6), channel_id=1, source_target_pairs={{0,15},{1,0},{2,1},{3,2},{4,3},{5,4},{6,5},{7,6},{8,7},{9,8},{10,9... | collective-permute-start | bytes 24584 | tf_op jit(solution)/shard_map/ppermute | solution.py:10
  141.7 17.3 %collective-permute-start.15 = (bf16[32,128]{1,0:T(8,128)(2,1)S(1)}, bf16[32,128]{1,0:T(8,128)(2,1)S(1)}, u32[]{:S(2)}, u32[]{:S(2)}) collective-permute-start(bf16[32,128]{1,0:T(8,128)(2,1)S(1)} %broadcast_select_fusion.4), channel_id=1, source_target_pairs={{0,2},{1,3},{2,4},{3,5},{4,6},{5,7},{6,8},{7,9},{8,10},{9,11},{10,... | collective-permute-start | bytes 24584 | tf_op jit(solution)/shard_map/ppermute | solution.py:10
  141.7 17.3 %collective-permute-start.16 = (bf16[32,128]{1,0:T(8,128)(2,1)S(1)}, bf16[32,128]{1,0:T(8,128)(2,1)S(1)}, u32[]{:S(2)}, u32[]{:S(2)}) collective-permute-start(bf16[32,128]{1,0:T(8,128)(2,1)S(1)} %broadcast_select_fusion.2), channel_id=1, source_target_pairs={{0,14},{1,15},{2,0},{3,1},{4,2},{5,3},{6,4},{7,5},{8,6},{9,7},{10,... | collective-permute-start | bytes 24584 | tf_op jit(solution)/shard_map/ppermute | solution.py:10
  146.5 12.5 %collective-permute-start.17 = (bf16[32,128]{1,0:T(8,128)(2,1)S(1)}, bf16[32,128]{1,0:T(8,128)(2,1)S(1)}, u32[]{:S(2)}, u32[]{:S(2)}) collective-permute-start(bf16[32,128]{1,0:T(8,128)(2,1)S(1)} %broadcast_select_fusion), channel_id=1, source_target_pairs={{0,8},{1,9},{2,10},{3,11},{4,12},{5,13},{6,14},{7,15},{8,0},{9,1},... | collective-permute-start | bytes 24584 | tf_op jit(solution)/shard_map/ppermute | solution.py:10
  168.2 3.5 %copy-start.22 = (pred[3072]{0:T(1024)(128)(4,1)S(1)}, pred[3072]{0:T(1024)(128)(4,1)}, u32[]{:S(2)}) copy-start(pred[3072]{0:T(1024)(128)(4,1)} %compare_and_fusion) | copy-start | bytes 9220
  168.2 3.5 %copy-start.27 = (bf16[128,128]{1,0:T(8,128)(2,1)S(1)}, bf16[128,128]{1,0:T(8,128)(2,1)}, u32[]{:S(2)}) copy-start(bf16[128,128]{1,0:T(8,128)(2,1)} %param.45) | copy-start | bytes 98308
  175.9 18.9 %copy-start.7 = (f32[512,128]{1,0:T(8,128)S(1)}, f32[512,128]{1,0:T(8,128)}, u32[]{:S(2)}) copy-start(f32[512,128]{1,0:T(8,128)} %fusion.61) | copy-start | bytes 786436
  175.9 18.9 %copy-start.13 = (bf16[256,128]{1,0:T(8,128)(2,1)S(1)}, bf16[256,128]{1,0:T(8,128)(2,1)}, u32[]{:S(2)}) copy-start(bf16[256,128]{1,0:T(8,128)(2,1)} %param.46) | copy-start | bytes 196612
  175.9 18.9 %copy-start.28 = (bf16[128,128]{1,0:T(8,128)(2,1)S(1)}, bf16[128,128]{1,0:T(8,128)(2,1)}, u32[]{:S(2)}) copy-start(bf16[128,128]{1,0:T(8,128)(2,1)} %param.47) | copy-start | bytes 98308
where the time goes:
time: 199 us; the launch traced here: 196 us
  local copies, waits for them, and re-layouts  69.6 us (35%)
  other arithmetic  65.1 us (33%)
  starting transfers between devices  27.5 us (14%)
  matrix products  22.9 us (12%)
  waiting for transfers between devices  10.6 us (5%)
    scatter-add x3, other arithmetic, edge_pass(): jax.ops.segment_sum(new_edges.astype(jnp.float32), target, num_segments=n...  43.3 us
    gather x3, local copies, waits for them, and re-layouts, edge_pass(): receiver_rows = jnp.take(padded, target, axis=0)  27.1 us
    gather x3, local copies, waits for them, and re-layouts, edge_pass(): sender_rows = jnp.take(table, senders, axis=0)  23.9 us
    ppermute x12, starting transfers between devices, shifted_2(): return lax.ppermute(value, axis, pairs)  21.4 us
    gather x10, local copies, waits for them, and re-layouts, halo_table(): jnp.take(node_rows, halo_list[number * slot_rows:(number + 1) * slot_rows...  10.5 us
    ppermute x6, waiting for transfers between devices, swapped(): return lax.ppermute(block, axis, route)  8.29 us
    dot_general x3, matrix products, edge_pass(): jnp.dot(sender_rows, weight_in[row_width:2 * row_width], preferred_elemen...  7.73 us
    dot_general x3, matrix products, edge_pass(): jnp.dot(hidden, weight_out, preferred_element_type=jnp.float32)  6.55 us
  transfers between devices with their start and end apart: 18, of which 6 were waited for; matrix products, arithmetic and copies ran while one was open for 49% of the time, Pallas kernels for 0%

commit v1 on v0

v1 whole, which is shorter than its diff:
```python
import functools

import jax
import jax.numpy as jnp
from jax import lax
from jax.experimental import pallas as pl
from jax.experimental.pallas import tpu as pltpu
from jax.sharding import PartitionSpec as P

BF = jnp.bfloat16
F32 = jnp.float32
MESH = pl.DeviceIdType.MESH
LANES = 128
GROUP = 4


def round_up(value, unit):
    return -(-value // unit) * unit


def mm(left, right):
    return jnp.dot(left, right, preferred_element_type=F32)


def silu(value):
    half = 0.5 * value
    return half + half * jnp.tanh(half)


def centred_weight(weight):
    wide = weight.astype(F32)
    wide = wide - jnp.mean(wide, axis=-1, keepdims=True)
    high = wide.astype(BF)
    low = (wide - high.astype(F32)).astype(BF)
    return jnp.concatenate([high, low], axis=0)


def normed_product(hidden, weight_pair):
    shifted = mm(jnp.concatenate([hidden, hidden], axis=1), weight_pair)
    width = shifted.shape[1]
    average = jnp.full((width, width), 1.0 / width, BF)
    spread = mm((shifted * shifted).astype(BF), average)
    return shifted * lax.rsqrt(spread + 1e-05)


def spread_column(index_row):
    return jnp.broadcast_to(index_row, (LANES, LANES)).T


def one_hot_columns(index_row, count, first=0):
    column = spread_column(index_row)
    lane = lax.broadcasted_iota(jnp.int32, (LANES, LANES), 1)
    pieces = [
        (column == lane + (first + start)).astype(F32).astype(BF)
        for start in range(0, count, LANES)
    ]
    return jnp.concatenate(pieces, axis=1)


def one_hot_rows(index_row, count, first=0):
    row = lax.broadcasted_iota(jnp.int32, (count, LANES), 0) + first
    return (row == jnp.broadcast_to(index_row, (count, LANES))).astype(F32).astype(BF)


def node_update(nodes, summed, weight_in, weight_pair):
    both = jnp.concatenate([nodes, summed.astype(BF)], axis=1)
    hidden = silu(mm(both, weight_in)).astype(BF)
    return (nodes.astype(F32) + normed_product(hidden, weight_pair)).astype(BF)


def kernel(
    dom,
    slot,
    nodes_ref,
    edges_ref,
    cedges_ref,
    send_ref,
    recv_ref,
    halo_ref,
    parent_ref,
    csend_ref,
    crecv_ref,
    fei_ref,
    feo_ref,
    fni_ref,
    fno_ref,
    cei_ref,
    ceo_ref,
    cni_ref,
    cno_ref,
    sei_ref,
    seo_ref,
    sni_ref,
    sno_ref,
    out_ref,
    hot_s,
    hot_t,
    chot_s,
    chot_t,
    halo_hot,
    parent_hot,
    gathered,
    cgathered,
    new_edges,
    cnew_edges,
    halo_out,
    halo_in,
    parents_in,
    pool_out,
    pool_in,
    ctable,
    agg_out,
    agg_in,
    cnew,
    nodes_mid,
    send_sem,
    halo_sem,
    parent_sem,
    pool_sem,
    table_sem,
    agg_sem,
    cnew_sem,
):
    node_count = nodes_ref.shape[0]
    edge_count = edges_ref.shape[0]
    cedge_count = cedges_ref.shape[0]
    table_rows = hot_s.shape[1] - node_count
    quarter = node_count // GROUP
    me = lax.axis_index("dom")
    rank = lax.rem(me, GROUP)
    base = me - rank
    offsets = (1, -1, 2, -2, dom // 2)

    def away(offset):
        return lax.rem(me + (offset + dom), dom)

    def mate(step):
        return base + lax.rem(rank + step, GROUP)

    barrier = pltpu.get_barrier_semaphore()
    ahead = lax.rem(base + GROUP, dom)
    behind = lax.rem(base + dom - GROUP, dom)
    greeted = [away(offset) for offset in offsets] + [away(-(dom // 2))]
    greeted += [mate(step) for step in range(1, GROUP)]
    greeted += [ahead + step for step in range(GROUP)]
    greeted += [behind + step for step in range(GROUP)]
    for device in greeted:
        pl.semaphore_signal(barrier, inc=1, device_id={"dom": device}, device_id_type=MESH)

    started = []

    def send(source, target, send_at, recv, device):
        copy = pltpu.make_async_remote_copy(
            src_ref=source,
            dst_ref=target,
            send_sem=send_sem.at[send_at],
            recv_sem=recv,
            device_id={"dom": device},
            device_id_type=MESH,
        )
        copy.start()
        started.append(copy)
        return copy

    for block in range(halo_hot.shape[0] // LANES):
        halo_hot[block * LANES : (block + 1) * LANES, :] = one_hot_columns(
            halo_ref[block : block + 1, :], node_count
        )
    halo_out[0] = mm(halo_hot[...], nodes_ref[...]).astype(BF)

    pl.semaphore_wait(barrier, len(greeted))

    def send_halo(turn):
        copies = []
        for number, offset in enumerate(offsets):
            rows = pl.ds(number * slot, slot)
            copies.append(
                send(
                    halo_out.at[turn, rows],
                    halo_in.at[turn, rows],
                    turn * 5 + number,
                    halo_sem.at[turn, number],
                    away(offset),
                )
            )
        return copies

    first_halo = send_halo(0)
    parent_copies = [
        send(parent_ref, parents_in.at[step - 1], 10 + step - 1, parent_sem.at[step - 1], mate(step))
        for step in range(1, GROUP)
    ]

    def fine_hot(block, carry):
        rows = pl.ds(pl.multiple_of(block * LANES, LANES), LANES)
        sender = send_ref[pl.ds(block, 1), :]
        receiver = recv_ref[pl.ds(block, 1), :]
        hot_s[rows, :table_rows] = one_hot_columns(sender, table_rows)
        hot_s[rows, table_rows:] = one_hot_columns(receiver, node_count)
        hot_t[:, rows] = one_hot_rows(receiver, node_count)
        return carry

    def coarse_hot(block, carry):
        rows = pl.ds(pl.multiple_of(block * LANES, LANES), LANES)
        sender = csend_ref[pl.ds(block, 1), :]
        receiver = crecv_ref[pl.ds(block, 1), :]
        chot_s[rows, : 3 * node_count] = one_hot_columns(sender, 3 * node_count)
        chot_s[rows, 3 * node_count :] = one_hot_columns(receiver, node_count)
        chot_t[:, rows] = one_hot_rows(receiver, node_count)
        return carry

    lax.fori_loop(0, edge_count // LANES, fine_hot, 0)

    def edge_loop(source, hot, gathers, weight_in, weight_out, target, count):
        own = weight_in[:LANES, :]
        pair = centred_weight(weight_out[...])
        chunk = 512 if count % 512 == 0 else LANES

        def body(step, carry):
            rows = pl.ds(pl.multiple_of(step * chunk, chunk), chunk)
            old = source[rows, :]
            hidden = silu(mm(old, own) + mm(hot[rows, :], gathers[...])).astype(BF)
            target[rows, :] = (old.astype(F32) + normed_product(hidden, pair)).astype(BF)
            return carry

        lax.fori_loop(0, count // chunk, body, 0)

    def fine_step(turn, nodes, source, halo_copies, wei, weo, wni, wno):
        own = nodes[...]
        gathered[:node_count, :] = mm(own, wei[LANES : 2 * LANES, :]).astype(BF)
        gathered[table_rows:, :] = mm(own, wei[2 * LANES :, :]).astype(BF)
        filled = node_count + 5 * slot
        if filled < table_rows:
            gathered[filled:table_rows, :] = jnp.zeros((table_rows - filled, LANES), BF)
        for copy in halo_copies:
            copy.wait_recv()
        gathered[node_count:filled, :] = mm(
            halo_in[turn], wei[LANES : 2 * LANES, :]
        ).astype(BF)
        edge_loop(source, hot_s, gathered, wei, weo, new_edges, edge_count)
        summed = mm(hot_t[...], new_edges[...])
        return node_update(own, summed, wni[...], centred_weight(wno[...]))

    nodes_one = fine_step(
        0, nodes_ref, edges_ref, first_halo, fei_ref, feo_ref, fni_ref, fno_ref
    )
    nodes_mid[...] = nodes_one

    for block in range(node_count // LANES):
        span = slice(block * LANES, (block + 1) * LANES)
        parent_hot[:, span] = one_hot_rows(parent_ref[block : block + 1, :], node_count)
    pool_out[...] = mm(parent_hot[...], nodes_one).astype(BF)

    def scatter_quarters(outgoing, incoming, send_at, sems):
        copies = []
        for step in range(1, GROUP):
            rows = pl.ds(pl.multiple_of(lax.rem(rank + step, GROUP) * quarter, quarter), quarter)
            copies.append(
                send(outgoing.at[rows], incoming.at[step - 1], send_at + step - 1, sems.at[step - 1], mate(step))
            )
        return copies

    mine = pl.ds(pl.multiple_of(rank * quarter, quarter), quarter)

    def quarter_sum(outgoing, incoming, copies):
        total = outgoing[mine, :].astype(F32)
        for copy in copies:
            copy.wait_recv()
        for step in range(GROUP - 1):
            total = total + incoming[step].astype(F32)
        return total

    pool_copies = scatter_quarters(pool_out, pool_in, 13, pool_sem)
    lax.fori_loop(0, cedge_count // LANES, coarse_hot, 0)
    for copy in parent_copies:
        copy.wait_recv()
    marks = []
    for source in [parent_ref] + [parents_in.at[step] for step in range(GROUP - 1)]:
        marks += [
            one_hot_rows(source[block : block + 1, :], quarter, rank * quarter)
            for block in range(node_count // LANES)
        ]
    marks = jnp.concatenate(marks, axis=1)
    children = mm(marks, jnp.ones((marks.shape[1], LANES), BF))
    pooled = quarter_sum(pool_out, pool_in, pool_copies)
    ctable[mine, :] = (pooled / children).astype(BF)

    def table_send(number, region, device):
        rows = pl.ds(pl.multiple_of(region * node_count + rank * quarter, quarter), quarter)
        return send(ctable.at[mine], ctable.at[rows], 16 + number, table_sem.at[number], device)

    table_copies = []
    for step in range(1, GROUP):
        table_copies.append(table_send(step - 1, 0, mate(step)))
    for step in range(GROUP):
        to = lax.rem(rank + step, GROUP)
        table_copies.append(table_send(3 + step, 1, ahead + to))
        table_copies.append(table_send(7 + step, 2, behind + to))

    for copy in table_copies[: GROUP - 1]:
        copy.wait_recv()
    own_coarse = ctable[:node_count, :]
    sender_weight = cei_ref[LANES : 2 * LANES, :]
    cgathered[:node_count, :] = mm(own_coarse, sender_weight).astype(BF)
    cgathered[3 * node_count :, :] = mm(own_coarse, cei_ref[2 * LANES :, :]).astype(BF)
    for copy in table_copies[GROUP - 1 :]:
        copy.wait_recv()
    cgathered[node_count : 3 * node_count, :] = mm(
        ctable[node_count:, :], sender_weight
    ).astype(BF)
    edge_loop(cedges_ref, chot_s, cgathered, cei_ref, ceo_ref, cnew_edges, cedge_count)
    agg_out[...] = mm(chot_t[...], cnew_edges[...]).astype(BF)
    agg_copies = scatter_quarters(agg_out, agg_in, 27, agg_sem)
    for block in range(node_count // LANES):
        parent_hot[block * LANES : (block + 1) * LANES, :] = one_hot_columns(
            parent_ref[block : block + 1, :], node_count
        )
    coarse_sum = quarter_sum(agg_out, agg_in, agg_copies)
    cnew[mine, :] = node_update(
        ctable[mine, :], coarse_sum, cni_ref[...], centred_weight(cno_ref[...])
    )
    new_copies = [
        send(cnew.at[mine], cnew.at[mine], 30 + step - 1, cnew_sem.at[step - 1], mate(step))
        for step in range(1, GROUP)
    ]
    for copy in new_copies:
        copy.wait_recv()

    lifted = mm(parent_hot[...], cnew[...])
    middle = (nodes_mid[...].astype(F32) + lifted).astype(BF)
    nodes_mid[...] = middle
    halo_out[1] = mm(halo_hot[...], middle).astype(BF)
    second_halo = send_halo(1)
    out_ref[...] = fine_step(
        1, nodes_mid, new_edges, second_halo, sei_ref, seo_ref, sni_ref, sno_ref
    )
    for copy in started:
        copy.wait_send()


def on_device(*arrays):
    (nodes, edges, cedges, senders, receivers, halo, parent, csenders, creceivers) = arrays[:9]
    weights = arrays[9:]
    dom = lax.axis_size("dom")
    node_count, width = nodes.shape
    edge_count = edges.shape[0]
    cedge_count = cedges.shape[0]
    slot = halo.shape[0] // 5
    halo_rows = round_up(halo.shape[0], LANES)
    table_rows = round_up(node_count + 5 * slot, 256)
    quarter = node_count // GROUP
    halo = jnp.pad(halo, (0, halo_rows - halo.shape[0]))
    rows = lambda index: index.reshape(-1, LANES)
    operands = [nodes, edges, cedges] + [
        rows(index) for index in (senders, receivers, halo, parent, csenders, creceivers)
    ]
    operands += list(weights)
    dma = pltpu.SemaphoreType.DMA
    scratch = [
        pltpu.VMEM((edge_count, table_rows + node_count), BF),
        pltpu.VMEM((node_count, edge_count), BF),
        pltpu.VMEM((cedge_count, 4 * node_count), BF),
        pltpu.VMEM((node_count, cedge_count), BF),
        pltpu.VMEM((halo_rows, node_count), BF),
        pltpu.VMEM((node_count, node_count), BF),
        pltpu.VMEM((table_rows + node_count, width), BF),
        pltpu.VMEM((4 * node_count, width), BF),
        pltpu.VMEM((edge_count, width), BF),
        pltpu.VMEM((cedge_count, width), BF),
        pltpu.VMEM((2, halo_rows, width), BF),
        pltpu.VMEM((2, 5 * slot, width), BF),
        pltpu.VMEM((GROUP - 1, node_count // LANES, LANES), jnp.int32),
        pltpu.VMEM((node_count, width), BF),
        pltpu.VMEM((GROUP - 1, quarter, width), BF),
        pltpu.VMEM((3 * node_count, width), BF),
        pltpu.VMEM((node_count, width), BF),
        pltpu.VMEM((GROUP - 1, quarter, width), BF),
        pltpu.VMEM((node_count, width), BF),
        pltpu.VMEM((node_count, width), BF),
        dma((33,)),
        dma((2, 5)),
        dma((GROUP - 1,)),
        dma((GROUP - 1,)),
        dma((11,)),
        dma((GROUP - 1,)),
        dma((GROUP - 1,)),
    ]
    vmem = pl.BlockSpec(memory_space=pltpu.VMEM)
    return pl.pallas_call(
        functools.partial(kernel, dom, slot),
        out_shape=jax.ShapeDtypeStruct((node_count, width), BF),
        in_specs=[vmem] * len(operands),
        out_specs=vmem,
        scratch_shapes=scratch,
        compiler_params=pltpu.CompilerParams(
            collective_id=0, has_side_effects=True, vmem_limit_bytes=48 * 1024 * 1024
        ),
        cost_estimate=pl.CostEstimate(
            flops=2 * 10**10, bytes_accessed=3 * 10**6, transcendentals=2 * 10**6
        ),
        name="multiscale_block",
    )(*operands)


def solution(mesh):
    rows = P(("grp", "dom"), None)
    flat = P(("grp", "dom"))
    placed = (rows,) * 3 + (flat,) * 6 + (P(),) * 12
    return jax.shard_map(
        on_device, mesh=mesh, in_specs=placed, out_specs=rows, check_vma=False
    )
```

time: 199 us -> 69.3 us (0.35)
  other arithmetic: 65.1 us -> 0 us
  local copies, waits for them, and re-layouts: 69.6 us -> 16.2 us
  Pallas kernels: 0 us -> 52 us
  starting transfers between devices: 27.5 us -> 0 us
  matrix products: 22.9 us -> 0 us
  waiting for transfers between devices: 10.6 us -> 0 us
    gather x17 -> x0, local copies, waits for them, and re-layouts: 62.8 us -> none  [the longest x3 27.1 us: edge_pass(): receiver_rows = jnp.take(padded, target, axis=0)]
    pallas_call x0 -> x1, Pallas kernels: none -> 52 us  [on_device(): pl.pallas_call(functools.partial(kernel, dom, slot), out_shape=jax.ShapeD...]
    scatter-add x5 -> x0, other arithmetic: 49.7 us -> none  [the longest x3 43.3 us: edge_pass(): jax.ops.segment_sum(new_edges.astype(jnp.float32), target, num_segments=n...]
    ppermute x18 -> x0, starting transfers between devices: 27.5 us -> none  [the longest x12 21.4 us: shifted_2(): return lax.ppermute(value, axis, pairs)]
    dot_general x15 -> x0, matrix products: 22.9 us -> none  [the longest x3 7.73 us: edge_pass(): jnp.dot(sender_rows, weight_in[row_width:2 * row_width], preferred_elemen...]
    unnamed x70 -> x43, local copies, waits for them, and re-layouts: 3.73 us -> 16.2 us
    ppermute x18 -> x0, waiting for transfers between devices: 10.6 us -> none  [the longest x6 8.29 us: swapped(): return lax.ppermute(block, axis, route)]
    and x6 -> x0, other arithmetic: 4.94 us -> none  [the longest x2 2.57 us: edge_pass(): receiver_rows = jnp.take(padded, target, axis=0)]
  transfers between devices with their start and end apart: 18 -> 0, of which waited for: 6 -> 0; matrix products, arithmetic and copies ran while one was open for 49% -> 0% of each run, Pallas kernels for 0% -> 0%
where the time goes in v1:
time: 69.3 us; the launch traced here: 68.3 us
  Pallas kernels  52 us (75%)
  local copies, waits for them, and re-layouts  16.2 us (23%)
    pallas_call x1, Pallas kernels, on_device(): pl.pallas_call(functools.partial(kernel, dom, slot), out_shape=jax.ShapeD...  52 us
    unnamed x43, local copies, waits for them, and re-layouts  16.2 us

profile of v1, /device:TPU:0, one launch (start us, length us, event | category | flops | bytes accessed | tf_op | source)
XLA Modules:
  0.0 68.3 jit_solution(8901239139329459509)
XLA Ops:
  0.0 0.0 copy-start.17
  0.0 0.0 copy-start.20
  0.0 0.0 copy-start.19
  0.0 0.7 %copy-done.20 = s32[160]{0:T(256)S(1)} copy-done((s32[160]{0:T(256)S(1)}, s32[160]{0:T(256)}, u32[]{:S(2)}) %copy-start.20) | copy-done | bytes 664
  0.7 0.0 copy-done.17
  0.7 0.0 copy-done.19
  0.7 0.0 copy-start
  0.7 1.1 %copy-done = bf16[3072,128]{1,0:T(8,128)(2,1)S(1)} copy-done((bf16[3072,128]{1,0:T(8,128)(2,1)S(1)}, bf16[3072,128]{1,0:T(8,128)(2,1)}, u32[]{:S(2)}) %copy-start) | copy-done | bytes 786456
  1.8 0.0 copy-start.1
  1.9 1.0 %copy-done.1 = bf16[1536,128]{1,0:T(8,128)(2,1)S(1)} copy-done((bf16[1536,128]{1,0:T(8,128)(2,1)S(1)}, bf16[1536,128]{1,0:T(8,128)(2,1)}, u32[]{:S(2)}) %copy-start.1) | copy-done | bytes 393240
  2.8 0.0 copy-start.2
  2.8 0.9 %copy-done.2 = bf16[512,128]{1,0:T(8,128)(2,1)S(1)} copy-done((bf16[512,128]{1,0:T(8,128)(2,1)S(1)}, bf16[512,128]{1,0:T(8,128)(2,1)}, u32[]{:S(2)}) %copy-start.2) | copy-done | bytes 131096
  3.7 0.0 copy-start.3
  3.8 0.9 %copy-done.3 = bf16[384,128]{1,0:T(8,128)(2,1)S(1)} copy-done((bf16[384,128]{1,0:T(8,128)(2,1)S(1)}, bf16[384,128]{1,0:T(8,128)(2,1)}, u32[]{:S(2)}) %copy-start.3) | copy-done | bytes 98328
  4.6 0.0 copy-start.4
  4.6 0.9 %copy-done.4 = bf16[384,128]{1,0:T(8,128)(2,1)S(1)} copy-done((bf16[384,128]{1,0:T(8,128)(2,1)S(1)}, bf16[384,128]{1,0:T(8,128)(2,1)}, u32[]{:S(2)}) %copy-start.4) | copy-done | bytes 98328
  5.5 0.0 copy-start.5
  5.5 0.9 %copy-done.5 = bf16[384,128]{1,0:T(8,128)(2,1)S(1)} copy-done((bf16[384,128]{1,0:T(8,128)(2,1)S(1)}, bf16[384,128]{1,0:T(8,128)(2,1)}, u32[]{:S(2)}) %copy-start.5) | copy-done | bytes 98328
  6.4 0.0 copy-start.6
  6.4 0.8 %copy-done.6 = bf16[256,128]{1,0:T(8,128)(2,1)S(1)} copy-done((bf16[256,128]{1,0:T(8,128)(2,1)S(1)}, bf16[256,128]{1,0:T(8,128)(2,1)}, u32[]{:S(2)}) %copy-start.6) | copy-done | bytes 65560
  7.3 0.0 copy-start.7
  7.3 0.8 %copy-done.7 = bf16[256,128]{1,0:T(8,128)(2,1)S(1)} copy-done((bf16[256,128]{1,0:T(8,128)(2,1)S(1)}, bf16[256,128]{1,0:T(8,128)(2,1)}, u32[]{:S(2)}) %copy-start.7) | copy-done | bytes 65560
  8.1 0.0 copy-start.8
  8.1 0.8 %copy-done.8 = bf16[256,128]{1,0:T(8,128)(2,1)S(1)} copy-done((bf16[256,128]{1,0:T(8,128)(2,1)S(1)}, bf16[256,128]{1,0:T(8,128)(2,1)}, u32[]{:S(2)}) %copy-start.8) | copy-done | bytes 65560
  8.9 0.0 copy-start.9
  9.0 0.8 %copy-done.9 = bf16[128,128]{1,0:T(8,128)(2,1)S(1)} copy-done((bf16[128,128]{1,0:T(8,128)(2,1)S(1)}, bf16[128,128]{1,0:T(8,128)(2,1)}, u32[]{:S(2)}) %copy-start.9) | copy-done | bytes 32792
  9.7 0.0 copy-start.10
  9.7 0.8 %copy-done.10 = bf16[128,128]{1,0:T(8,128)(2,1)S(1)} copy-done((bf16[128,128]{1,0:T(8,128)(2,1)S(1)}, bf16[128,128]{1,0:T(8,128)(2,1)}, u32[]{:S(2)}) %copy-start.10) | copy-done | bytes 32792
  10.5 0.0 copy-start.11
  10.5 0.8 %copy-done.11 = bf16[128,128]{1,0:T(8,128)(2,1)S(1)} copy-done((bf16[128,128]{1,0:T(8,128)(2,1)S(1)}, bf16[128,128]{1,0:T(8,128)(2,1)}, u32[]{:S(2)}) %copy-start.11) | copy-done | bytes 32792
  11.2 0.0 copy-start.12
  11.2 0.8 %copy-done.12 = bf16[128,128]{1,0:T(8,128)(2,1)S(1)} copy-done((bf16[128,128]{1,0:T(8,128)(2,1)S(1)}, bf16[128,128]{1,0:T(8,128)(2,1)}, u32[]{:S(2)}) %copy-start.12) | copy-done | bytes 32792
  12.0 0.0 copy-start.13
  12.0 0.8 %copy-done.13 = bf16[128,128]{1,0:T(8,128)(2,1)S(1)} copy-done((bf16[128,128]{1,0:T(8,128)(2,1)S(1)}, bf16[128,128]{1,0:T(8,128)(2,1)}, u32[]{:S(2)}) %copy-start.13) | copy-done | bytes 32792
  12.7 0.0 copy-start.14
  12.7 0.8 %copy-done.14 = bf16[128,128]{1,0:T(8,128)(2,1)S(1)} copy-done((bf16[128,128]{1,0:T(8,128)(2,1)S(1)}, bf16[128,128]{1,0:T(8,128)(2,1)}, u32[]{:S(2)}) %copy-start.14) | copy-done | bytes 32792
  13.5 0.0 copy-start.15
  13.5 0.7 %copy-done.15 = s32[3072]{0:T(1024)S(1)} copy-done((s32[3072]{0:T(1024)S(1)}, s32[3072]{0:T(1024)}, u32[]{:S(2)}) %copy-start.15) | copy-done | bytes 12312
  14.2 0.0 copy-start.16
  14.2 0.7 %copy-done.16 = s32[3072]{0:T(1024)S(1)} copy-done((s32[3072]{0:T(1024)S(1)}, s32[3072]{0:T(1024)}, u32[]{:S(2)}) %copy-start.16) | copy-done | bytes 12312
  14.9 0.0 copy-start.18
  14.9 0.7 %copy-done.18 = s32[1536]{0:T(1024)S(1)} copy-done((s32[1536]{0:T(1024)S(1)}, s32[1536]{0:T(1024)}, u32[]{:S(2)}) %copy-start.18) | copy-done | bytes 6168
  15.6 52.0 %multiscale_block.1 = bf16[512,128]{1,0:T(8,128)(2,1)S(1)} custom-call(bf16[512,128]{1,0:T(8,128)(2,1)S(1)} %copy-done.2, bf16[3072,128]{1,0:T(8,128)(2,1)S(1)} %copy-done, bf16[1536,128]{1,0:T(8,128)(2,1)S(1)} %copy-done.1, s32[24,128]{1,0:T(8,128)S(1)} %bitcast.7, s32[24,128]{1,0:T(8,128)S(1)} %bitcast.8, s32[2,128]{1,0:T(2,128)S(1)} %pad_bitcast_fusion.halo_ref, ...), custom_call_target="tpu_custom_call" | custom-call | flops 20000000000 | bytes 3000000 | tf_op jit(solution)/shard_map/multiscale_block/pallas_call | solution.py:389
  67.6 0.7 copy.23
  (1 shorter events, 0.0 us)
Async XLA Ops:
  0.0 0.7 %copy-start.17 = (s32[1536]{0:T(1024)S(1)}, s32[1536]{0:T(1024)}, u32[]{:S(2)}) copy-start(s32[1536]{0:T(1024)} %param.28) | copy-start | bytes 18436
  0.0 0.7 %copy-start.20 = (s32[160]{0:T(256)S(1)}, s32[160]{0:T(256)}, u32[]{:S(2)}) copy-start(s32[160]{0:T(256)} %param.26) | copy-start | bytes 1924
  0.0 0.7 %copy-start.19 = (s32[512]{0:T(512)S(1)}, s32[512]{0:T(512)}, u32[]{:S(2)}) copy-start(s32[512]{0:T(512)} %param.27) | copy-start | bytes 6148
  0.7 1.1 %copy-start = (bf16[3072,128]{1,0:T(8,128)(2,1)S(1)}, bf16[3072,128]{1,0:T(8,128)(2,1)}, u32[]{:S(2)}) copy-start(bf16[3072,128]{1,0:T(8,128)(2,1)} %edges_ref.1) | copy-start | bytes 2359300
  1.8 1.0 %copy-start.1 = (bf16[1536,128]{1,0:T(8,128)(2,1)S(1)}, bf16[1536,128]{1,0:T(8,128)(2,1)}, u32[]{:S(2)}) copy-start(bf16[1536,128]{1,0:T(8,128)(2,1)} %cedges_ref.1) | copy-start | bytes 1179652
  2.8 0.9 %copy-start.2 = (bf16[512,128]{1,0:T(8,128)(2,1)S(1)}, bf16[512,128]{1,0:T(8,128)(2,1)}, u32[]{:S(2)}) copy-start(bf16[512,128]{1,0:T(8,128)(2,1)} %nodes_ref.1) | copy-start | bytes 393220
  3.7 0.9 %copy-start.3 = (bf16[384,128]{1,0:T(8,128)(2,1)S(1)}, bf16[384,128]{1,0:T(8,128)(2,1)}, u32[]{:S(2)}) copy-start(bf16[384,128]{1,0:T(8,128)(2,1)} %fei_ref.1) | copy-start | bytes 294916
  4.6 0.9 %copy-start.4 = (bf16[384,128]{1,0:T(8,128)(2,1)S(1)}, bf16[384,128]{1,0:T(8,128)(2,1)}, u32[]{:S(2)}) copy-start(bf16[384,128]{1,0:T(8,128)(2,1)} %cei_ref.1) | copy-start | bytes 294916
  5.5 0.9 %copy-start.5 = (bf16[384,128]{1,0:T(8,128)(2,1)S(1)}, bf16[384,128]{1,0:T(8,128)(2,1)}, u32[]{:S(2)}) copy-start(bf16[384,128]{1,0:T(8,128)(2,1)} %sei_ref.1) | copy-start | bytes 294916
  6.4 0.8 %copy-start.6 = (bf16[256,128]{1,0:T(8,128)(2,1)S(1)}, bf16[256,128]{1,0:T(8,128)(2,1)}, u32[]{:S(2)}) copy-start(bf16[256,128]{1,0:T(8,128)(2,1)} %fni_ref.1) | copy-start | bytes 196612
  7.3 0.8 %copy-start.7 = (bf16[256,128]{1,0:T(8,128)(2,1)S(1)}, bf16[256,128]{1,0:T(8,128)(2,1)}, u32[]{:S(2)}) copy-start(bf16[256,128]{1,0:T(8,128)(2,1)} %cni_ref.1) | copy-start | bytes 196612
  8.1 0.8 %copy-start.8 = (bf16[256,128]{1,0:T(8,128)(2,1)S(1)}, bf16[256,128]{1,0:T(8,128)(2,1)}, u32[]{:S(2)}) copy-start(bf16[256,128]{1,0:T(8,128)(2,1)} %sni_ref.1) | copy-start | bytes 196612
  8.9 0.8 %copy-start.9 = (bf16[128,128]{1,0:T(8,128)(2,1)S(1)}, bf16[128,128]{1,0:T(8,128)(2,1)}, u32[]{:S(2)}) copy-start(bf16[128,128]{1,0:T(8,128)(2,1)} %feo_ref.1) | copy-start | bytes 98308
  9.7 0.8 %copy-start.10 = (bf16[128,128]{1,0:T(8,128)(2,1)S(1)}, bf16[128,128]{1,0:T(8,128)(2,1)}, u32[]{:S(2)}) copy-start(bf16[128,128]{1,0:T(8,128)(2,1)} %fno_ref.1) | copy-start | bytes 98308
  10.5 0.8 %copy-start.11 = (bf16[128,128]{1,0:T(8,128)(2,1)S(1)}, bf16[128,128]{1,0:T(8,128)(2,1)}, u32[]{:S(2)}) copy-start(bf16[128,128]{1,0:T(8,128)(2,1)} %ceo_ref.1) | copy-start | bytes 98308
  11.2 0.8 %copy-start.12 = (bf16[128,128]{1,0:T(8,128)(2,1)S(1)}, bf16[128,128]{1,0:T(8,128)(2,1)}, u32[]{:S(2)}) copy-start(bf16[128,128]{1,0:T(8,128)(2,1)} %cno_ref.1) | copy-start | bytes 98308
  12.0 0.8 %copy-start.13 = (bf16[128,128]{1,0:T(8,128)(2,1)S(1)}, bf16[128,128]{1,0:T(8,128)(2,1)}, u32[]{:S(2)}) copy-start(bf16[128,128]{1,0:T(8,128)(2,1)} %seo_ref.1) | copy-start | bytes 98308
  12.7 0.8 %copy-start.14 = (bf16[128,128]{1,0:T(8,128)(2,1)S(1)}, bf16[128,128]{1,0:T(8,128)(2,1)}, u32[]{:S(2)}) copy-start(bf16[128,128]{1,0:T(8,128)(2,1)} %sno_ref.1) | copy-start | bytes 98308
  13.5 0.7 %copy-start.15 = (s32[3072]{0:T(1024)S(1)}, s32[3072]{0:T(1024)}, u32[]{:S(2)}) copy-start(s32[3072]{0:T(1024)} %param.24) | copy-start | bytes 36868
  14.2 0.7 %copy-start.16 = (s32[3072]{0:T(1024)S(1)}, s32[3072]{0:T(1024)}, u32[]{:S(2)}) copy-start(s32[3072]{0:T(1024)} %param.25) | copy-start | bytes 36868
  14.9 0.7 %copy-start.18 = (s32[1536]{0:T(1024)S(1)}, s32[1536]{0:T(1024)}, u32[]{:S(2)}) copy-start(s32[1536]{0:T(1024)} %param.29) | copy-start | bytes 18436

commit v2 on v1

--- a/solution.py
+++ b/solution.py
@@ -12,6 +12,8 @@
 MESH = pl.DeviceIdType.MESH
 LANES = 128
 GROUP = 4
+ARGUMENTS = 21
+LOAD_ORDER = (0, 5, 6, 3, 4, 1, 9, 10, 11, 12, 7, 8, 2) + tuple(range(13, 21))
 
 
 def round_up(value, unit):
@@ -71,56 +73,75 @@
 def kernel(
     dom,
     slot,
-    nodes_ref,
-    edges_ref,
-    cedges_ref,
-    send_ref,
-    recv_ref,
-    halo_ref,
-    parent_ref,
-    csend_ref,
-    crecv_ref,
-    fei_ref,
-    feo_ref,
-    fni_ref,
-    fno_ref,
-    cei_ref,
-    ceo_ref,
-    cni_ref,
-    cno_ref,
-    sei_ref,
-    seo_ref,
-    sni_ref,
-    sno_ref,
-    out_ref,
-    hot_s,
-    hot_t,
-    chot_s,
-    chot_t,
-    halo_hot,
-    parent_hot,
-    gathered,
-    cgathered,
-    new_edges,
-    cnew_edges,
-    halo_out,
-    halo_in,
-    parents_in,
-    pool_out,
-    pool_in,
-    ctable,
-    agg_out,
-    agg_in,
-    cnew,
-    nodes_mid,
-    send_sem,
-    halo_sem,
-    parent_sem,
-    pool_sem,
-    table_sem,
-    agg_sem,
-    cnew_sem,
+    *refs,
 ):
+    given = refs[:ARGUMENTS]
+    out_ref = refs[ARGUMENTS]
+    local = refs[ARGUMENTS + 1 : 2 * ARGUMENTS + 1]
+    (
+        nodes_ref,
+        edges_ref,
+        cedges_ref,
+        send_ref,
+        recv_ref,
+        halo_ref,
+        parent_ref,
+        csend_ref,
+        crecv_ref,
+        fei_ref,
+        feo_ref,
+        fni_ref,
+        fno_ref,
+        cei_ref,
+        ceo_ref,
+        cni_ref,
+        cno_ref,
+        sei_ref,
+        seo_ref,
+        sni_ref,
+        sno_ref,
+    ) = local
+    (
+        hot_s,
+        hot_t,
+        chot_s,
+        chot_t,
+        halo_hot,
+        parent_hot,
+        gathered,
+        cgathered,
+        new_edges,
+        cnew_edges,
+        halo_out,
+        halo_in,
+        parents_in,
+        pool_out,
+        pool_in,
+        ctable,
+        agg_out,
+        agg_in,
+        cnew,
+        nodes_mid,
+        send_sem,
+        halo_sem,
+        parent_sem,
+        pool_sem,
+        table_sem,
+        agg_sem,
+        cnew_sem,
+        load_sem,
+    ) = refs[2 * ARGUMENTS + 1 :]
+    loads = [
+        pltpu.make_async_copy(source, target, load_sem.at[number])
+        for number, (source, target) in enumerate(zip(given, local))
+    ]
+    for number in LOAD_ORDER:
+        loads[number].start()
+
+    def arrived(numbers):
+        for number in numbers:
+            loads[number].wait()
+
     node_count = nodes_ref.shape[0]
     edge_count = edges_ref.shape[0]
     cedge_count = cedges_ref.shape[0]
@@ -162,6 +183,7 @@
         started.append(copy)
         return copy
 
+    arrived((0, 5, 6))
     for block in range(halo_hot.shape[0] // LANES):
         halo_hot[block * LANES : (block + 1) * LANES, :] = one_hot_columns(
             halo_ref[block : block + 1, :], node_count
@@ -209,7 +231,9 @@
         chot_t[:, rows] = one_hot_rows(receiver, node_count)
         return carry
 
+    arrived((3, 4))
     lax.fori_loop(0, edge_count // LANES, fine_hot, 0)
+    arrived((1, 2, 7, 8) + tuple(range(9, 21)))
 
     def edge_loop(source, hot, gathers, weight_in, weight_out, target, count):
         own = weight_in[:LANES, :]
@@ -356,7 +380,8 @@
     ]
     operands += list(weights)
     dma = pltpu.SemaphoreType.DMA
-    scratch = [
+    scratch = [pltpu.VMEM(operand.shape, operand.dtype) for operand in operands]
+    scratch += [
         pltpu.VMEM((edge_count, table_rows + node_count), BF),
         pltpu.VMEM((node_count, edge_count), BF),
         pltpu.VMEM((cedge_count, 4 * node_count), BF),
@@ -384,16 +409,17 @@
         dma((11,)),
         dma((GROUP - 1,)),
         dma((GROUP - 1,)),
+        dma((ARGUMENTS,)),
     ]
     vmem = pl.BlockSpec(memory_space=pltpu.VMEM)
     return pl.pallas_call(
         functools.partial(kernel, dom, slot),
         out_shape=jax.ShapeDtypeStruct((node_count, width), BF),
-        in_specs=[vmem] * len(operands),
+        in_specs=[pl.BlockSpec(memory_space=pltpu.HBM)] * len(operands),
         out_specs=vmem,
         scratch_shapes=scratch,
         compiler_params=pltpu.CompilerParams(
-            collective_id=0, has_side_effects=True, vmem_limit_bytes=48 * 1024 * 1024
+            collective_id=0, has_side_effects=True, vmem_limit_bytes=60 * 1024 * 1024
         ),
         cost_estimate=pl.CostEstimate(
             flops=2 * 10**10, bytes_accessed=3 * 10**6, transcendentals=2 * 10**6

time: 69.3 us -> 56 us (0.81); the launches traced: 68.3 us -> 55.8 us
  local copies, waits for them, and re-layouts: 16.2 us -> 2.81 us
  Pallas kernels: 52 us -> 53 us
    unnamed x43 -> x3, local copies, waits for them, and re-layouts: 16.2 us -> 2.25 us
    pallas_call x1, Pallas kernels: 52 us -> 53 us  [on_device(): pl.pallas_call(functools.partial(kernel, dom, slot), out_shape=jax.ShapeD...]
where the time goes in v2:
time: 56 us; the launch traced here: 55.8 us
  Pallas kernels  53 us (95%)
  local copies, waits for them, and re-layouts  2.81 us (5%)
    pallas_call x1, Pallas kernels, on_device(): pl.pallas_call(functools.partial(kernel, dom, slot), out_shape=jax.ShapeD...  53 us
    unnamed x3, local copies, waits for them, and re-layouts  2.25 us

profile of v2, /device:TPU:0, one launch (start us, length us, event | category | flops | bytes accessed | tf_op | source)
XLA Modules:
  0.0 55.8 jit_solution(614849820051778786)
XLA Ops:
  0.0 0.0 copy-start
  0.0 0.7 %copy-done = s32[160]{0:T(256)S(1)} copy-done((s32[160]{0:T(256)S(1)}, s32[160]{0:T(256)}, u32[]{:S(2)}) %copy-start) | copy-done | bytes 664
  0.7 0.6 %pad_bitcast_fusion.refs_5_ = s32[2,128]{1,0:T(2,128)} fusion(s32[160]{0:T(256)S(1)} %copy-done), kind=kLoop, calls=%fused_computation | loop fusion | bytes 1664 | tf_op jit(solution)/shard_map/reshape | solution.py:377
  1.2 53.0 %multiscale_block.1 = bf16[512,128]{1,0:T(8,128)(2,1)} custom-call(bf16[512,128]{1,0:T(8,128)(2,1)} %refs_0_.1, bf16[3072,128]{1,0:T(8,128)(2,1)} %refs_1_.1, bf16[1536,128]{1,0:T(8,128)(2,1)} %refs_2_.1, s32[24,128]{1,0:T(8,128)} %bitcast.7, s32[24,128]{1,0:T(8,128)} %bitcast.8, s32[2,128]{1,0:T(2,128)} %pad_bitcast_fusion.refs_5_, s32[4,128]{1,0:T(4,128)} %bitcast.11, ...), custom_call_target="tpu_custom_call" | custom-call | flops 20000000000 | bytes 3000000 | tf_op jit(solution)/shard_map/multiscale_block/pallas_call | solution.py:415
  54.3 1.6 %copy.23 = bf16[512,128]{1,0:T(8,128)(2,1)} copy(bf16[512,128]{1,0:T(8,128)(2,1)} %multiscale_block.1) | data formatting | bytes 262144
Async XLA Ops:
  0.0 0.7 %copy-start = (s32[160]{0:T(256)S(1)}, s32[160]{0:T(256)}, u32[]{:S(2)}) copy-start(s32[160]{0:T(256)} %param.26) | copy-start | bytes 1924

commit v3 on v2

--- a/solution.py
+++ b/solution.py
@@ -316,10 +316,15 @@
     table_copies = []
     for step in range(1, GROUP):
         table_copies.append(table_send(step - 1, 0, mate(step)))
-    for step in range(GROUP):
-        to = lax.rem(rank + step, GROUP)
-        table_copies.append(table_send(3 + step, 1, ahead + to))
-        table_copies.append(table_send(7 + step, 2, behind + to))
+    far_copies = [table_send(3, 1, ahead + rank), table_send(4, 2, behind + rank)]
+    for region, far in enumerate(far_copies, 1):
+        far.wait_recv()
+        rows = pl.ds(pl.multiple_of(region * node_count + rank * quarter, quarter), quarter)
+        for step in range(1, GROUP):
+            number = 1 + 3 * region + step
+            table_copies.append(
+                send(ctable.at[rows], ctable.at[rows], 16 + number, table_sem.at[number], mate(step))
+            )
 
     for copy in table_copies[: GROUP - 1]:
         copy.wait_recv()

time: 56 us -> 54.6 us (0.975)
  Pallas kernels: 53 us -> 51.6 us
    pallas_call x1, Pallas kernels: 53 us -> 51.6 us  [on_device(): pl.pallas_call(functools.partial(kernel, dom, slot), out_shape=jax.ShapeD...]
where the time goes in v3:
time: 54.6 us; the launch traced here: 54.4 us
  Pallas kernels  51.6 us (95%)
  local copies, waits for them, and re-layouts  2.81 us (5%)
    pallas_call x1, Pallas kernels, on_device(): pl.pallas_call(functools.partial(kernel, dom, slot), out_shape=jax.ShapeD...  51.6 us
    unnamed x3, local copies, waits for them, and re-layouts  2.25 us

profile of v3, /device:TPU:0, one launch (start us, length us, event | category | flops | bytes accessed | tf_op | source)
XLA Modules:
  0.0 54.4 jit_solution(16516327559665305764)
XLA Ops:
  0.0 0.0 copy-start
  0.0 0.7 %copy-done = s32[160]{0:T(256)S(1)} copy-done((s32[160]{0:T(256)S(1)}, s32[160]{0:T(256)}, u32[]{:S(2)}) %copy-start) | copy-done | bytes 664
  0.7 0.6 %pad_bitcast_fusion.refs_5_ = s32[2,128]{1,0:T(2,128)} fusion(s32[160]{0:T(256)S(1)} %copy-done), kind=kLoop, calls=%fused_computation | loop fusion | bytes 1664 | tf_op jit(solution)/shard_map/reshape | solution.py:382
  1.2 51.6 %multiscale_block.1 = bf16[512,128]{1,0:T(8,128)(2,1)} custom-call(bf16[512,128]{1,0:T(8,128)(2,1)} %refs_0_.1, bf16[3072,128]{1,0:T(8,128)(2,1)} %refs_1_.1, bf16[1536,128]{1,0:T(8,128)(2,1)} %refs_2_.1, s32[24,128]{1,0:T(8,128)} %bitcast.7, s32[24,128]{1,0:T(8,128)} %bitcast.8, s32[2,128]{1,0:T(2,128)} %pad_bitcast_fusion.refs_5_, s32[4,128]{1,0:T(4,128)} %bitcast.11, ...), custom_call_target="tpu_custom_call" | custom-call | flops 20000000000 | bytes 3000000 | tf_op jit(solution)/shard_map/multiscale_block/pallas_call | solution.py:420
  52.9 1.6 %copy.23 = bf16[512,128]{1,0:T(8,128)(2,1)} copy(bf16[512,128]{1,0:T(8,128)(2,1)} %multiscale_block.1) | data formatting | bytes 262144
Async XLA Ops:
  0.0 0.7 %copy-start = (s32[160]{0:T(256)S(1)}, s32[160]{0:T(256)}, u32[]{:S(2)}) copy-start(s32[160]{0:T(256)} %param.26) | copy-start | bytes 1924
